TPU v7x, 128 devices: a whole 4x4x4 slice. The times are simulated.
128 devices in a mesh: ja: 8 (over x, core), ka: 16 (over z, y).
Axes of the slice: x: 4, y: 4, z: 4, core: 2. Of those that a mesh axis runs over, the one named last changes fastest.
Arguments:
- blocks: bfloat16 [512, 128, 128, 128], P(('ja', 'ka')), may hold values from -6 to 6
- coords: int32 [512, 3], P(('ja', 'ka')), may hold values from 0 to 127, as said below
- live_counts: int32 [128], P(('ja', 'ka')), may hold values from 1 to 4, as said below
- mode2_factor: bfloat16 [16384, 512], P(('ja', 'ka')), may hold values from -0.52734375 to 0.52734375
- mode3_factor: bfloat16 [16384, 512], P(('ka', 'ja')), may hold values from -0.52734375 to 0.52734375
Outputs:
- mttkrp: float32 [2048, 512], P(('ja', 'ka'))
Inputs may be any that keep to these rules, and one draw needn't show every extreme that they name: `coords`: column 0 lies in 0 to 15 and favours some popular row blocks. The device at index j of ja and k of ka holds slots whose column 1 lies in j * 16 to (j + 1) * 16 - 1 and whose column 2 lies in k * 8 to (k + 1) * 8 - 1. `live_counts`: slots of a device beyond its count are dead; some device in every draw has all 4 slots live.
All inputs are finite; a program needn't handle non-finite values.
Results may differ from a plain program's by a relative error of at most 0.0003.
Values may be sent and summed in bfloat16 or wider, within the bound.
A program may use at most 64 MiB of HBM per device.

v0:
```python
import jax
import jax.numpy as jnp
from jax import lax
from jax.sharding import PartitionSpec as P

IROWS_DEV = 16


def block_product(block_cube, mode2_rows, mode3_rows):
    contracted = jnp.einsum(
        "abc,cr->abr", block_cube, mode3_rows, preferred_element_type=jnp.float32
    )
    return jnp.einsum("abr,br->ar", contracted, mode2_rows.astype(jnp.float32))


def on_device(blocks, coords, live_counts, mode2_factor, mode3_factor):
    block_edge = blocks.shape[1]
    rank_width = mode2_factor.shape[1]
    mode2_panel = lax.all_gather(mode2_factor, "ka", axis=0, tiled=True)
    mode3_panel = lax.all_gather(mode3_factor, "ja", axis=0, tiled=True)
    mode2_start = lax.axis_index("ja") * mode2_panel.shape[0]
    mode3_start = lax.axis_index("ka") * mode3_panel.shape[0]
    column_count = lax.axis_size("ja")
    within_count = lax.axis_size("ka")
    total_rows = IROWS_DEV * column_count * within_count

    def slot_rows_of(slot_index):
        block_cube = lax.dynamic_index_in_dim(blocks, slot_index, 0, keepdims=False)
        position = lax.dynamic_index_in_dim(coords, slot_index, 0, keepdims=False)
        mode2_rows = lax.dynamic_slice_in_dim(
            mode2_panel, position[1] * block_edge - mode2_start, block_edge, 0
        )
        mode3_rows = lax.dynamic_slice_in_dim(
            mode3_panel, position[2] * block_edge - mode3_start, block_edge, 0
        )
        return (block_product(block_cube, mode2_rows, mode3_rows), position[0] * block_edge)

    def add_block(slot_index, running):
        block_rows, row_start = slot_rows_of(slot_index)
        current = lax.dynamic_slice_in_dim(running, row_start, block_rows.shape[0], 0)
        return lax.dynamic_update_slice_in_dim(running, current + block_rows, row_start, 0)

    totals = jnp.zeros((total_rows, rank_width), jnp.float32)
    totals = lax.fori_loop(jnp.int32(0), live_counts[0], add_block, totals)
    owned = lax.psum_scatter(totals, ("ja", "ka"), scatter_dimension=0, tiled=True)
    return owned


def solution(mesh):
    placed = (
        P(("ja", "ka"), None, None, None),
        P(("ja", "ka"), None),
        P(("ja", "ka")),
        P(("ja", "ka"), None),
        P(("ka", "ja"), None),
    )
    return jax.shard_map(
        on_device, mesh=mesh, in_specs=placed, out_specs=P(("ja", "ka"), None), check_vma=False
    )
```

profile of v0, /device:TPU:0, one launch (start us, length us, event | category | flops | bytes accessed | tf_op | source)
XLA Modules:
  0.0 787.6 jit_solution(4829204910456181342)
XLA Ops:
  6.5 0.0 all-gather.5.cloned.1.call-start
  6.5 0.7 all-gather.5.cloned.1.call-update
  7.3 0.0 all-gather.3.cloned.1.call-start
  7.3 0.7 all-gather.3.cloned.1.call-update
  8.0 0.0 reduce-scatter.2.cloned.1.call-start
  8.1 26.8 %all-gather.5.cloned.1.call-done = bf16[1024,512]{1,0:T(8,128)(2,1)} async-done(((bf16[128,512]{1,0:T(8,128)(2,1)}), bf16[1024,512]{1,0:T(8,128)(2,1)}) %all-gather.5.cloned.1.call-update) | async-done | bytes 1048592 | tf_op jit(solution)/shard_map/all_gather | solution.py:20
  34.9 47.4 %all-gather.3.cloned.1.call-done = bf16[2048,512]{1,0:T(8,128)(2,1)} async-done(((bf16[128,512]{1,0:T(8,128)(2,1)}), bf16[2048,512]{1,0:T(8,128)(2,1)}) %all-gather.3.cloned.1.call-update) | async-done | bytes 2097168 | tf_op jit(solution)/shard_map/all_gather | solution.py:19
  82.2 2.5 broadcast_in_dim.3
  84.7 54.1 %while.10 = (s32[]{:T(128)}, f32[2048,512]{1,0:T(8,128)}, s32[]{:T(128)}, s32[4,3]{1,0:T(4,128)}, s32[]{:T(128)}, /*index=5*/bf16[2048,512]{1,0:T(8,128)(2,1)}, ...) while((s32[]{:T(128)}, f32[2048,512]{1,0:T(8,128)}, ...), condition=%wide.region_1.2_spmd, body=%wide.region_0.1_spmd.sunk | while | flops 2164326400 | bytes 6029725 | solution.py:44
  85.4 0.7 constant_dynamic-slice_fusion.2
  86.1 0.7 fusion.13
  88.7 0.9 bitcast_convert_fusion.2
  89.6 6.8 multiply_reduce_fusion.2
  96.4 1.7 fusion.14
  98.7 0.7 constant_dynamic-slice_fusion.2
  99.4 0.7 fusion.13
  102.0 0.9 bitcast_convert_fusion.2
  103.0 6.8 multiply_reduce_fusion.2
  109.7 1.7 fusion.14
  112.1 0.7 constant_dynamic-slice_fusion.2
  112.8 0.7 fusion.13
  115.4 0.9 bitcast_convert_fusion.2
  116.3 6.8 multiply_reduce_fusion.2
  123.1 1.7 fusion.14
  125.4 0.7 constant_dynamic-slice_fusion.2
  126.1 0.7 fusion.13
  128.7 0.9 bitcast_convert_fusion.2
  129.7 6.8 multiply_reduce_fusion.2
  136.4 1.7 fusion.14
  138.8 0.0 reduce-scatter.2.cloned.1.call-update
  138.8 642.3 %reduce-scatter.2.cloned.1.call-done = f32[16,512]{1,0:T(8,128)} async-done(((f32[2048,512]{1,0:T(8,128)}), f32[16,512]{1,0:T(8,128)}) %reduce-scatter.2.cloned.1.call-update) | async-done | bytes 32784 | tf_op jit(solution)/shard_map/reduce_scatter | solution.py:45
Async XLA Ops:
  6.5 28.4 %all-gather.5.cloned.1.call-start = ((), (), s32[]{:S(2)}) async-start(), calls=%async_computation.2 | async-start | bytes 1179648 | tf_op jit(solution)/shard_map/all_gather | solution.py:20
  7.3 75.0 %all-gather.3.cloned.1.call-start = ((), (), s32[]{:S(2)}) async-start(), calls=%async_computation.1 | async-start | bytes 2228224 | tf_op jit(solution)/shard_map/all_gather | solution.py:19
  8.0 773.1 %reduce-scatter.2.cloned.1.call-start = ((), (), s32[]{:S(2)}) async-start(), calls=%async_computation.3 | async-start | bytes 4227072 | tf_op jit(solution)/shard_map/reduce_scatter | solution.py:45
Sparse Core Ops, SparseCore 0:
  9.1 25.7 all-gather.4
  37.0 45.1 all-gather.2
  138.9 642.1 reduce-scatter.1
where the time goes:
time: 788 us
  waiting for transfers between devices  718 us (91%)
  matrix products  27 us (3%)
  between operations  13.1 us (2%)
  loops' own time  11.2 us (1%)
  other arithmetic  10.5 us (1%)
    reduce_scatter x1, waiting for transfers between devices, on_device(): lax.psum_scatter(totals, ('ja', 'ka'), scatter_dimension=0, tiled=True)  642 us
    all_gather x1, waiting for transfers between devices, on_device(): mode2_panel = lax.all_gather(mode2_factor, 'ka', axis=0, tiled=True)  47.4 us
    dot_general x4, matrix products, block_product(): jnp.einsum('abc,cr->abr', block_cube, mode3_rows, preferred_element_type=...  27 us
    all_gather x1, waiting for transfers between devices, on_device(): mode3_panel = lax.all_gather(mode3_factor, 'ja', axis=0, tiled=True)  26.8 us
  transfers between devices with their start and end apart: 3, of which 3 were waited for; matrix products, arithmetic and copies ran while one was open for 0% of the time, Pallas kernels for 0%

commit v1 on v0

--- a/solution.py
+++ b/solution.py
@@ -17,7 +17,15 @@
     block_edge = blocks.shape[1]
     rank_width = mode2_factor.shape[1]
     mode2_panel = lax.all_gather(mode2_factor, "ka", axis=0, tiled=True)
-    mode3_panel = lax.all_gather(mode3_factor, "ja", axis=0, tiled=True)
+    ways, here = (lax.axis_size("ja"), lax.axis_index("ja"))
+    grown, reach = (mode3_factor, 1)
+    while reach < ways:
+        theirs = lax.ppermute(grown, "ja", [(d, d ^ reach) for d in range(ways)])
+        mine_first = jnp.concatenate([grown, theirs], axis=0)
+        theirs_first = jnp.concatenate([theirs, grown], axis=0)
+        grown = jnp.where(here & reach == 0, mine_first, theirs_first)
+        reach = 2 * reach
+    mode3_panel = grown
     mode2_start = lax.axis_index("ja") * mode2_panel.shape[0]
     mode3_start = lax.axis_index("ka") * mode3_panel.shape[0]
     column_count = lax.axis_size("ja")

time: 788 us -> 764 us (0.970)
  waiting for transfers between devices: 718 us -> 686 us
    all_gather x1 -> x0, waiting for transfers between devices: 26.8 us -> none  [on_device(): mode3_panel = lax.all_gather(mode3_factor, 'ja', axis=0, tiled=True)]
    all_gather x1, waiting for transfers between devices: 47.4 us -> 23.5 us  [on_device(): mode2_panel = lax.all_gather(mode2_factor, 'ka', axis=0, tiled=True)]
    ppermute x0 -> x3, waiting for transfers between devices: none -> 19.9 us  [on_device(): theirs = lax.ppermute(grown, 'ja', [(d, d ^ reach) for d in range(ways)])]
  transfers between devices with their start and end apart: 3 -> 5, of which waited for: 3 -> 5; matrix products, arithmetic and copies ran while one was open for 0% -> 0% of each run, Pallas kernels for 0% -> 0%
where the time goes in v1:
time: 764 us
  waiting for transfers between devices  686 us (90%)
  matrix products  28.5 us (4%)
  between operations  13.4 us (2%)
  other arithmetic  12.2 us (2%)
  loops' own time  10.7 us (1%)
  local copies, waits for them, and re-layouts  7.69 us (1%)
    reduce_scatter x1, waiting for transfers between devices, on_device(): lax.psum_scatter(totals, ('ja', 'ka'), scatter_dimension=0, tiled=True)  642 us
    dot_general x4, matrix products, block_product(): jnp.einsum('abc,cr->abr', block_cube, mode3_rows, preferred_element_type=...  28.5 us
    all_gather x1, waiting for transfers between devices, on_device(): mode2_panel = lax.all_gather(mode2_factor, 'ka', axis=0, tiled=True)  23.5 us
    ppermute x3, waiting for transfers between devices, on_device(): theirs = lax.ppermute(grown, 'ja', [(d, d ^ reach) for d in range(ways)])  19.9 us
  transfers between devices with their start and end apart: 5, of which 5 were waited for; matrix products, arithmetic and copies ran while one was open for 0% of the time, Pallas kernels for 0%

profile of v1, /device:TPU:0, one launch (start us, length us, event | category | flops | bytes accessed | tf_op | source)
XLA Modules:
  0.0 763.7 jit_solution(2276227115890258184)
XLA Ops:
  6.5 0.7 all-gather.2.cloned.1.call-update
  7.4 1.5 collective-permute-done
  8.9 1.0 maximum_select_fusion.2
  10.0 1.7 collective-permute-start.1
  11.6 6.8 collective-permute-done.1
  18.6 3.2 collective-permute-start.2
  21.8 11.5 %collective-permute-done.2 = bf16[512,512]{1,0:T(8,128)(2,1)S(1)} collective-permute-done((bf16[512,512]{1,0:T(8,128)(2,1)S(1)}, bf16[512,512]{1,0:T(8,128)(2,1)S(1)}, u32[]{:S(2)}, u32[]{:S(2)}) %collective-permute-start.2) | collective-permute-done | bytes 524320 | tf_op jit(solution)/shard_map/ppermute | solution.py:23
  33.4 0.5 maximum_select_fusion
  33.8 23.5 %all-gather.2.cloned.1.call-done = bf16[2048,512]{1,0:T(8,128)(2,1)} async-done(((bf16[128,512]{1,0:T(8,128)(2,1)}), bf16[2048,512]{1,0:T(8,128)(2,1)}) %all-gather.2.cloned.1.call-update) | async-done | bytes 2097168 | tf_op jit(solution)/shard_map/all_gather | solution.py:19
  57.3 2.5 broadcast_in_dim.3
  59.8 54.9 %while.10 = (s32[]{:T(128)}, f32[2048,512]{1,0:T(8,128)}, s32[]{:T(128)}, s32[4,3]{1,0:T(4,128)}, s32[]{:T(128)}, /*index=5*/bf16[2048,512]{1,0:T(8,128)(2,1)}, ...) while((s32[]{:T(128)}, f32[2048,512]{1,0:T(8,128)}, ...), condition=%wide.region_1.2_spmd, body=%wide.region_0.1_spmd.sunk | while | flops 2164326400 | bytes 6029725 | solution.py:52
  60.4 0.7 constant_dynamic-slice_fusion.2
  61.1 0.6 fusion.13
  63.6 0.9 bitcast_convert_fusion.2
  64.5 7.1 multiply_reduce_fusion.2
  71.6 1.7 fusion.14
  74.0 0.7 constant_dynamic-slice_fusion.2
  74.7 0.6 fusion.13
  77.1 0.9 bitcast_convert_fusion.2
  78.1 7.1 multiply_reduce_fusion.2
  85.2 1.7 fusion.14
  87.5 0.7 constant_dynamic-slice_fusion.2
  88.2 0.6 fusion.13
  90.7 0.9 bitcast_convert_fusion.2
  91.6 7.1 multiply_reduce_fusion.2
  98.7 1.7 fusion.14
  101.1 0.7 constant_dynamic-slice_fusion.2
  101.8 0.6 fusion.13
  104.2 0.9 bitcast_convert_fusion.2
  105.2 7.1 multiply_reduce_fusion.2
  112.3 1.7 fusion.14
  114.7 642.2 %reduce-scatter.2.cloned.1.call-done = f32[16,512]{1,0:T(8,128)} async-done(((f32[2048,512]{1,0:T(8,128)}), f32[16,512]{1,0:T(8,128)}) %reduce-scatter.2.cloned.1.call-update) | async-done | bytes 32784 | tf_op jit(solution)/shard_map/reduce_scatter | solution.py:53
  (5 shorter events, 0.4 us)
Async XLA Ops:
  6.5 50.8 %all-gather.2.cloned.1.call-start = ((), (), s32[]{:S(2)}) async-start(), calls=%async_computation.1 | async-start | bytes 2228224 | tf_op jit(solution)/shard_map/all_gather | solution.py:19
  7.3 749.6 %reduce-scatter.2.cloned.1.call-start = ((), (), s32[]{:S(2)}) async-start(), calls=%async_computation.2 | async-start | bytes 4227072 | tf_op jit(solution)/shard_map/reduce_scatter | solution.py:53
  7.3 1.6 collective-permute-start
  10.0 8.4 %collective-permute-start.1 = (bf16[256,512]{1,0:T(8,128)(2,1)S(1)}, bf16[256,512]{1,0:T(8,128)(2,1)S(1)}, u32[]{:S(2)}, u32[]{:S(2)}) collective-permute-start(bf16[256,512]{1,0:T(8,128)(2,1)S(1)} %maximum_select_fusion.2), channel_id=1, source_target_pairs={{0,32},{16,48},{32,0},{48,16},{64,96},{80,112},{96,64},{112,80},{1... | collective-permute-start | bytes 786440 | tf_op jit(solution)/shard_map/ppermute | solution.py:23
  18.6 14.7 %collective-permute-start.2 = (bf16[512,512]{1,0:T(8,128)(2,1)S(1)}, bf16[512,512]{1,0:T(8,128)(2,1)S(1)}, u32[]{:S(2)}, u32[]{:S(2)}) collective-permute-start(bf16[512,512]{1,0:T(8,128)(2,1)S(1)} %maximum_select_fusion.1), channel_id=1, source_target_pairs={{0,64},{16,80},{32,96},{48,112},{64,0},{80,16},{96,32},{112,48},{1... | collective-permute-start | bytes 1572872 | tf_op jit(solution)/shard_map/ppermute | solution.py:23
Sparse Core Ops, SparseCore 0:
  9.5 47.7 all-gather.1
  114.8 642.0 reduce-scatter.1

commit v2 on v0

--- a/solution.py
+++ b/solution.py
@@ -16,7 +16,9 @@
 def on_device(blocks, coords, live_counts, mode2_factor, mode3_factor):
     block_edge = blocks.shape[1]
     rank_width = mode2_factor.shape[1]
-    mode2_panel = lax.all_gather(mode2_factor, "ka", axis=0, tiled=True)
+    mode2_panel = jnp.concatenate(
+        lax.all_to_all(jnp.stack([mode2_factor] * lax.axis_size("ka")), "ka", 0, 0), axis=0
+    )
     mode3_panel = lax.all_gather(mode3_factor, "ja", axis=0, tiled=True)
     mode2_start = lax.axis_index("ja") * mode2_panel.shape[0]
     mode3_start = lax.axis_index("ka") * mode3_panel.shape[0]

time: 788 us -> 751 us (0.953)
  waiting for transfers between devices: 718 us -> 674 us
  starting transfers between devices: 0.08 us -> 8.21 us
    all_gather x1 -> x0, waiting for transfers between devices: 47.4 us -> none  [on_device(): mode2_panel = lax.all_gather(mode2_factor, 'ka', axis=0, tiled=True)]
    all_to_all x0 -> x1, starting transfers between devices: none -> 8.13 us  [on_device(): lax.all_to_all(jnp.stack([mode2_factor] * lax.axis_size('ka')), 'ka', 0, 0)]
where the time goes in v2:
time: 751 us
  waiting for transfers between devices  674 us (90%)
  matrix products  27 us (4%)
  between operations  13.4 us (2%)
  loops' own time  11.3 us (2%)
  local copies, waits for them, and re-layouts  10.4 us (1%)
  starting transfers between devices  8.21 us (1%)
    reduce_scatter x1, waiting for transfers between devices, on_device(): lax.psum_scatter(totals, ('ja', 'ka'), scatter_dimension=0, tiled=True)  642 us
    dot_general x4, matrix products, block_product(): jnp.einsum('abc,cr->abr', block_cube, mode3_rows, preferred_element_type=...  27 us
    all_gather x1, waiting for transfers between devices, on_device(): mode3_panel = lax.all_gather(mode3_factor, 'ja', axis=0, tiled=True)  26.7 us
  transfers between devices with their start and end apart: 3, of which 3 were waited for; matrix products, arithmetic and copies ran while one was open for 0% of the time, Pallas kernels for 0%

profile of v2, /device:TPU:0, one launch (start us, length us, event | category | flops | bytes accessed | tf_op | source)
XLA Modules:
  0.0 750.9 jit_solution(13115198360363826081)
XLA Ops:
  6.5 2.4 stack.2
  9.0 8.1 %all-to-all-start = ((bf16[16,128,512]{2,1,0:T(8,128)(2,1)}), bf16[16,128,512]{2,1,0:T(8,128)(2,1)S(1)}, u32[]{:S(2)}, u32[]{:S(2)}) async-start(bf16[16,128,512]{2,1,0:T(8,128)(2,1)} %stack.2), calls=%async_computation | async-start | bytes 4194304 | tf_op jit(solution)/shard_map/all_to_all | solution.py:20
  17.1 0.0 all-gather.2.cloned.1.call-start
  17.2 0.7 all-gather.2.cloned.1.call-update
  17.8 0.0 reduce-scatter.2.cloned.1.call-start
  17.9 26.7 %all-gather.2.cloned.1.call-done = bf16[1024,512]{1,0:T(8,128)(2,1)} async-done(((bf16[128,512]{1,0:T(8,128)(2,1)}), bf16[1024,512]{1,0:T(8,128)(2,1)}) %all-gather.2.cloned.1.call-update) | async-done | bytes 1048592 | tf_op jit(solution)/shard_map/all_gather | solution.py:22
  44.6 4.2 all-to-all-done
  48.8 2.5 broadcast_in_dim.3
  51.2 50.7 %while.10 = (s32[]{:T(128)}, f32[2048,512]{1,0:T(8,128)}, s32[]{:T(128)}, s32[4,3]{1,0:T(4,128)}, s32[]{:T(128)}, /*index=5*/bf16[2048,512]{1,0:T(8,128)(2,1)S(1...) while((s32[]{:T(128)}, f32[2048,512]{1,0:T(8,128)}, ...), condition=%wide.region_1.2_spmd, body=%wide.region_0.1_spmd.sunk | while | flops 2164326400 | bytes 6029725 | solution.py:46
  51.9 0.7 constant_dynamic-slice_fusion.2
  52.6 0.7 fusion.13
  55.3 6.8 multiply_reduce_fusion.2
  62.0 1.7 fusion.14
  64.4 0.7 constant_dynamic-slice_fusion.2
  65.1 0.7 fusion.13
  67.8 6.8 multiply_reduce_fusion.2
  74.5 1.7 fusion.14
  76.9 0.7 constant_dynamic-slice_fusion.2
  77.6 0.7 fusion.13
  80.3 6.8 multiply_reduce_fusion.2
  87.0 1.7 fusion.14
  89.4 0.7 constant_dynamic-slice_fusion.2
  90.1 0.7 fusion.13
  92.8 6.8 multiply_reduce_fusion.2
  99.6 1.7 fusion.14
  101.9 0.0 reduce-scatter.2.cloned.1.call-update
  101.9 642.1 %reduce-scatter.2.cloned.1.call-done = f32[16,512]{1,0:T(8,128)} async-done(((f32[2048,512]{1,0:T(8,128)}), f32[16,512]{1,0:T(8,128)}) %reduce-scatter.2.cloned.1.call-update) | async-done | bytes 32784 | tf_op jit(solution)/shard_map/reduce_scatter | solution.py:47
  (4 shorter events, 0.1 us)
Async XLA Ops:
  9.0 39.8 %all-to-all-start = ((bf16[16,128,512]{2,1,0:T(8,128)(2,1)}), bf16[16,128,512]{2,1,0:T(8,128)(2,1)S(1)}, u32[]{:S(2)}, u32[]{:S(2)}) async-start(bf16[16,128,512]{2,1,0:T(8,128)(2,1)} %stack.2), calls=%async_computation | async-start | bytes 4194304 | tf_op jit(solution)/shard_map/all_to_all | solution.py:20
  17.1 27.5 %all-gather.2.cloned.1.call-start = ((), (), s32[]{:S(2)}) async-start(), calls=%async_computation.2 | async-start | bytes 1179648 | tf_op jit(solution)/shard_map/all_gather | solution.py:22
  17.8 726.2 %reduce-scatter.2.cloned.1.call-start = ((), (), s32[]{:S(2)}) async-start(), calls=%async_computation.3 | async-start | bytes 4227072 | tf_op jit(solution)/shard_map/reduce_scatter | solution.py:47
Sparse Core Ops, SparseCore 0:
  19.7 24.8 all-gather.1
  102.1 641.9 reduce-scatter.1
